TPU v7x, 32 devices: a whole 2x2x4 slice. The times are simulated.
32 devices in a mesh: parts: 2 (over y), replica: 4 (over z), tensor: 4 (over x, core).
Axes of the slice: x: 2, y: 2, z: 4, core: 2. Of those that a mesh axis runs over, the one named last changes fastest.
Arguments:
- tokens: bfloat16 [4096, 8192], P(('parts', 'replica'), 'tensor'), parts along dimension 0, may hold values from -6 to 6
- value_weight: bfloat16 [8192, 512], P('tensor'), may hold values from -0.0625 to 0.0625
- down_factor: bfloat16 [256, 8192, 64], P(('parts', 'replica'), 'tensor'), parts along dimension 0, may hold values from -0.0625 to 0.0625
- up_factor: bfloat16 [256, 64, 512], P(('parts', 'replica'), None, 'tensor'), parts along dimension 0, may hold values from -0.75 to 0.75
- request_adapter: int32 [4096], P('parts'), parts along dimension 0, may hold values from 0 to 127, as said below
- adapter_slot_map: int32 [256], P('parts'), parts along dimension 0, may hold values from 0 to 127, as said below
Outputs:
- values_out: bfloat16 [4096, 512], P(('parts', 'replica'), 'tensor'), parts along dimension 0
There are 2 independent parts, one for each index of `parts`. A program takes and returns all parts, laid end to end along the dimension named above; an argument that names none is the same for every part. Nothing has to cross between parts.
Inputs may be any that keep to these rules, and one draw needn't show every extreme that they name: `request_adapter`: replica r holds requests r * 512 to (r + 1) * 512 - 1, and pool slots r * 32 to (r + 1) * 32 - 1. Of the requests of one replica, at most 256 have adapters whose slots lie on one replica; in every draw some replicas receive exactly 256 from every replica. `adapter_slot_map`: A permutation.
All inputs are finite; a program needn't handle non-finite values.
Results may differ from a plain program's by a relative error of at most 0.0043.
Values may be sent and summed in bfloat16 or wider, within the bound.
No kernel may reach another device: no remote copies, remote signals or barrier semaphores. Data moves between devices by JAX's collectives and lax.ppermute only.
A program may use at most 128 MiB of HBM per device.

v0:
```python
import jax
import jax.numpy as jnp
from jax import lax
from jax.sharding import PartitionSpec as P

ADAPTER_SCALE = 0.5


def body(tokens, value_weight, down_factor, up_factor, request_adapter, adapter_slot_map):
    row_count, quarter = tokens.shape
    owners = lax.axis_size("replica")
    local_adapters = down_factor.shape[0]
    output_piece = up_factor.shape[2]
    capacity = 2 * row_count // owners
    my_index = lax.axis_index("replica")
    pool_slot = jnp.take(adapter_slot_map, request_adapter)
    owner_grid = (pool_slot // local_adapters).reshape(owners, row_count)
    local_grid = (pool_slot % local_adapters).reshape(owners, row_count)
    my_owner = lax.dynamic_slice_in_dim(owner_grid, my_index, 1, 0)[0]
    owner_hot = (my_owner[:, None] == jnp.arange(owners)[None, :]).astype(jnp.int32)
    my_rank = jnp.sum(jnp.cumsum(owner_hot, axis=0) * owner_hot, axis=1) - 1
    position = my_owner * capacity + my_rank
    packer = (jnp.arange(owners * capacity)[:, None] == position[None, :]).astype(jnp.bfloat16)
    outgoing = jnp.dot(packer, tokens, preferred_element_type=jnp.float32).astype(jnp.bfloat16)
    outgoing = outgoing.reshape(owners, capacity, quarter)
    partial_base = jnp.dot(tokens, value_weight, preferred_element_type=jnp.float32)
    arrived = lax.all_to_all(outgoing, "replica", split_axis=0, concat_axis=0, tiled=True)
    mine = (owner_grid == my_index).astype(jnp.int32)
    recv_rank = jnp.cumsum(mine, axis=1) - 1
    selector = (
        (recv_rank[:, None, :] == jnp.arange(capacity)[None, :, None]) & (mine[:, None, :] > 0)
    ).astype(jnp.int32)
    slot_local = jnp.sum(selector * local_grid[:, None, :], axis=2).reshape(owners * capacity)
    sort_order = jnp.argsort(slot_local, stable=True)
    inverse_order = jnp.argsort(sort_order)
    group_row_count = jnp.sum(
        (slot_local[:, None] == jnp.arange(local_adapters)[None, :]).astype(jnp.int32), axis=0
    )
    rows_by_adapter = jnp.take(arrived.reshape(owners * capacity, quarter), sort_order, axis=0)
    partial_rank = lax.ragged_dot(
        rows_by_adapter, down_factor, group_row_count, preferred_element_type=jnp.float32
    )
    rank_total = lax.psum(partial_rank, "tensor")
    local_base_output = None
    rank_projected = rank_total.astype(jnp.bfloat16)
    sorted_delta = lax.ragged_dot(
        rank_projected, up_factor, group_row_count, preferred_element_type=jnp.float32
    ).astype(jnp.bfloat16)
    adapter_delta = jnp.take(sorted_delta, inverse_order, axis=0).reshape(
        owners, capacity, output_piece
    )
    returned = lax.all_to_all(adapter_delta, "replica", split_axis=0, concat_axis=0, tiled=True)
    adapter_delta_rows = jnp.einsum(
        "pr,po->ro",
        packer,
        returned.reshape(owners * capacity, output_piece),
        preferred_element_type=jnp.float32,
    )
    local_base_output = lax.psum_scatter(partial_base, "tensor", scatter_dimension=1, tiled=True)
    return (local_base_output + ADAPTER_SCALE * adapter_delta_rows).astype(jnp.bfloat16)


def solution(mesh):
    in_specs = (
        P(("parts", "replica"), "tensor"),
        P("tensor", None),
        P(("parts", "replica"), "tensor", None),
        P(("parts", "replica"), None, "tensor"),
        P("parts"),
        P("parts"),
    )
    out_specs = P(("parts", "replica"), "tensor")
    return jax.shard_map(body, mesh=mesh, in_specs=in_specs, out_specs=out_specs, check_vma=False)
```

profile of v0, /device:TPU:0, one launch (start us, length us, event | category | flops | bytes accessed | tf_op | source)
XLA Modules:
  0.0 226.7 jit_solution(3690154552346166806)
XLA Ops:
  6.5 0.0 copy-start
  6.5 0.0 copy-start.1
  6.5 0.9 fusion.15
  7.4 0.0 copy-done.1
  7.4 0.0 copy-start.2
  7.4 12.6 %gather_fusion = s32[2048]{0:T(1024)S(1)} fusion(s32[128]{0:T(128)S(1)} %copy-done.1, s32[2048]{0:T(1024)S(1)} %fusion.15), kind=kCustom, calls=%fused_computation | custom fusion | bytes 24576 | tf_op jit(solution)/shard_map/jit(_take)/gather | solution.py:16
  20.0 0.0 copy-done.2
  20.1 1.2 reduce-window.14
  21.4 0.2 slice_reduce_fusion.1
  21.6 0.2 reduce-window.15
  21.8 0.1 add_bitcast_fusion.1
  21.9 0.0 copy-done
  21.9 4.3 %convolution_convert_fusion = bf16[1024,2048]{1,0:T(8,128)(2,1)} fusion(bf16[512,2048]{1,0:T(8,128)(2,1)S(1)} %copy-done, s32[512]{0:T(512)S(1)} %bitcast.49), kind=kOutput, calls=%fused_computation.4 | convolution fusion | flops 2150105088 | bytes 6293504 | tf_op jit(solution)/shard_map/dot_general | solution.py:24
  26.2 6.3 %all-to-all-start = ((bf16[4,256,2048]{2,1,0:T(8,128)(2,1)}), bf16[4,256,2048]{2,1,0:T(8,128)(2,1)}, u32[]{:S(2)}, u32[]{:S(2)}) async-start(bf16[4,256,2048]{2,1,0:T(8,128)(2,1)} %bitcast.36), calls=%async_computation.1 | async-start | bytes 8388608 | tf_op jit(solution)/shard_map/all_to_all | solution.py:27
  32.5 0.0 reduce-scatter.2.cloned.1.call-start
  32.5 3.9 %fusion.18 = f32[512,512]{1,0:T(8,128)} fusion(bf16[512,2048]{1,0:T(8,128)(2,1)S(1)} %copy-done, bf16[2048,512]{1,0:T(8,128)(2,1)} %param.7), kind=kOutput, calls=%fused_computation.59 | convolution fusion | flops 1073741824 | bytes 5242880 | tf_op jit(solution)/shard_map/dot_general | solution.py:26
  36.4 0.0 reduce-scatter.2.cloned.1.call-update
  36.5 1.2 reduce-window.16
  37.7 0.2 slice_reduce_fusion
  37.9 0.2 reduce-window.19
  38.1 0.1 add_bitcast_fusion
  38.2 0.5 select_reduce_fusion
  38.7 4.4 %sort.34 = (s32[1024]{0:T(1024)}, s32[1024]{0:T(1024)S(1)}) sort(s32[1024]{0:T(1024)S(1)} %bitcast.40, s32[1024]{0:T(1024)S(1)} %iota.28), dimensions={0}, to_apply=%region_7.8 | sort | flops 10240 | bytes 16384 | tf_op jit(solution)/shard_map/jit(argsort)/sort | solution.py:34
  43.1 4.4 %sort.35 = (s32[1024]{0:T(1024)}, s32[1024]{0:T(1024)S(1)}) sort(s32[1024]{0:T(1024)S(1)} %get-tuple-element.7, s32[1024]{0:T(1024)S(1)} %iota.29), dimensions={0}, to_apply=%region_8.9 | sort | flops 10240 | bytes 16384 | tf_op jit(solution)/shard_map/jit(argsort)/sort | solution.py:35
  47.5 0.6 convert_reduce_fusion
  48.1 2.4 %ragged-dot-metadata = (s32[33]{0:T(128)}, s32[35]{0:T(128)}, s32[35]{0:T(128)}, s32[1]{0:T(128)}) custom-call(s32[32]{0:T(128)} %convert_reduce_fusion), custom_call_target="tpu_custom_call" | custom-call | tf_op ragged-dot-metadata
  50.5 15.6 %copy.9 = bf16[32,2048,64]{2,1,0:T(8,128)(2,1)} copy(bf16[32,2048,64]{1,2,0:T(8,128)(2,1)} %param.8) | data formatting | bytes 16777216 | tf_op args[2]
  66.1 59.8 %all-to-all-done = bf16[4,256,2048]{2,1,0:T(8,128)(2,1)} async-done(((bf16[4,256,2048]{2,1,0:T(8,128)(2,1)}), bf16[4,256,2048]{2,1,0:T(8,128)(2,1)}, u32[]{:S(2)}, u32[]{:S(2)}) %all-to-all-start) | async-done | bytes 4194336 | tf_op jit(solution)/shard_map/all_to_all | solution.py:27
  125.9 11.6 %gather_fusion.1 = bf16[1024,2048]{1,0:T(8,128)(2,1)} fusion(bf16[1024,2048]{1,0:T(8,128)(2,1)} %bitcast.7, s32[1024]{0:T(1024)S(1)} %fusion.17), kind=kCustom, calls=%fused_computation.1 | custom fusion | bytes 8392704 | tf_op jit(solution)/shard_map/jit(_take)/gather | solution.py:39
  137.5 4.6 %broadcast_select_fusion = bf16[1024,2048]{1,0:T(8,128)(2,1)} fusion(bf16[1024,2048]{1,0:T(8,128)(2,1)} %gather_fusion.1, pred[1024]{0:T(1024)(128)(4,1)S(1)} %compare_and_fusion), kind=kLoop, calls=%fused_computation.3 | loop fusion | flops 2097152 | bytes 8389632 | tf_op jit(solution)/shard_map/jit(_take)/select_n | solution.py:39
  142.1 24.3 %ragged-dot-none.1 = f32[1024,64]{1,0:T(8,128)} custom-call(s32[1]{0:T(128)} %get-tuple-element.9, s32[33]{0:T(128)} %get-tuple-element.10, s32[35]{0:T(128)} %get-tuple-element.11, s32[35]{0:T(128)} %get-tuple-element.12, s32[1]{0:T(128)} %get-tuple-element.9, bf16[1024,2048]{1,0:T(8,128)(2,1)} %broadcast_select_fusion, bf16[32,2048,64]{2,1,0:T(8,128)(2,1)} %copy.9), custom_call_target="tpu_custom_call" | custom-call | flops 268435456 | bytes 12845184 | tf_op jit(solution)/shard_map/ragged_dot_general/ragged-dot-none
  166.4 17.7 %all-reduce.1 = bf16[1024,64]{1,0:T(8,128)(2,1)} all-reduce(f32[1024,64]{1,0:T(8,128)} %ragged-dot-none.1), channel_id=1, replica_groups=mesh['parts'=2,'replica'=4,'tensor'=4] {'tensor'}, use_global_device_ids=true, to_apply=%region_10.11 | all-reduce | flops 65536 | bytes 393216 | tf_op jit(solution)/shard_map/psum | solution.py:43
  184.2 15.3 %ragged-dot-none = f32[1024,128]{1,0:T(8,128)} custom-call(s32[1]{0:T(128)} %get-tuple-element.9, s32[33]{0:T(128)} %get-tuple-element.10, s32[35]{0:T(128)} %get-tuple-element.11, s32[35]{0:T(128)} %get-tuple-element.12, s32[1]{0:T(128)} %get-tuple-element.9, bf16[1024,64]{1,0:T(8,128)(2,1)} %all-reduce.1, bf16[32,64,128]{2,1,0:T(8,128)(2,1)} %param.9), custom_call_target="tpu_custom_call" | custom-call | flops 16777216 | bytes 1179776 | tf_op jit(solution)/shard_map/ragged_dot_general/ragged-dot-none
  199.5 1.1 convert_element_type.38
  200.6 3.2 %gather_fusion.2 = bf16[1024,128]{1,0:T(8,128)(2,1)S(1)} fusion(bf16[1024,128]{1,0:T(8,128)(2,1)S(1)} %convert_element_type.38, s32[1024]{0:T(1024)S(1)} %fusion.16), kind=kCustom, calls=%fused_computation.2 | custom fusion | bytes 528384 | tf_op jit(solution)/shard_map/jit(_take)/gather | solution.py:49
  203.8 0.9 broadcast_select_fusion.1
  204.7 3.4 %all-to-all-start.1 = ((bf16[4,256,128]{2,1,0:T(8,128)(2,1)}), bf16[4,256,128]{2,1,0:T(8,128)(2,1)S(1)}, u32[]{:S(2)}, u32[]{:S(2)}) async-start(bf16[4,256,128]{2,1,0:T(8,128)(2,1)} %broadcast_select_fusion.1), calls=%async_computation.2 | async-start | bytes 524288 | tf_op jit(solution)/shard_map/all_to_all | solution.py:52
  208.1 0.0 reduce-scatter.2.cloned.1.call-done
  208.1 9.3 %all-to-all-done.1 = bf16[4,256,128]{2,1,0:T(8,128)(2,1)S(1)} async-done(((bf16[4,256,128]{2,1,0:T(8,128)(2,1)}), bf16[4,256,128]{2,1,0:T(8,128)(2,1)S(1)}, u32[]{:S(2)}, u32[]{:S(2)}) %all-to-all-start.1) | async-done | bytes 262176 | tf_op jit(solution)/shard_map/all_to_all | solution.py:52
  217.5 2.4 %fusion.4 = bf16[512,128]{1,0:T(8,128)(2,1)} fusion(f32[512,128]{1,0:T(8,128)} %reduce-scatter.2.cloned.1.call-done, bf16[1024,128]{1,0:T(8,128)(2,1)S(1)} %bitcast.38, s32[512]{0:T(512)S(1)} %bitcast.50), kind=kOutput, calls=%fused_computation.12 | convolution fusion | flops 134938624 | bytes 657408 | tf_op jit(solution)/shard_map/pr,po->ro/dot_general | solution.py:53
  (19 shorter events, 0.2 us)
Async XLA Ops:
  6.5 15.4 %copy-start = (bf16[512,2048]{1,0:T(8,128)(2,1)S(1)}, bf16[512,2048]{1,0:T(8,128)(2,1)}, u32[]{:S(2)}) copy-start(bf16[512,2048]{1,0:T(8,128)(2,1)} %param.6) | copy-start | bytes 6291460
  6.5 0.9 copy-start.1
  7.4 12.6 %copy-start.2 = (s32[2048]{0:T(1024)S(1)}, s32[2048]{0:T(1024)}, u32[]{:S(2)}) copy-start(s32[2048]{0:T(1024)} %param.10) | copy-start | bytes 24580
  26.2 99.7 %all-to-all-start = ((bf16[4,256,2048]{2,1,0:T(8,128)(2,1)}), bf16[4,256,2048]{2,1,0:T(8,128)(2,1)}, u32[]{:S(2)}, u32[]{:S(2)}) async-start(bf16[4,256,2048]{2,1,0:T(8,128)(2,1)} %bitcast.36), calls=%async_computation.1 | async-start | bytes 8388608 | tf_op jit(solution)/shard_map/all_to_all | solution.py:27
  32.5 175.6 %reduce-scatter.2.cloned.1.call-start = ((), (), s32[]{:S(2)}) async-start(), calls=%async_computation.3 | async-start | bytes 1310720 | tf_op jit(solution)/shard_map/reduce_scatter | solution.py:59
  204.7 12.8 %all-to-all-start.1 = ((bf16[4,256,128]{2,1,0:T(8,128)(2,1)}), bf16[4,256,128]{2,1,0:T(8,128)(2,1)S(1)}, u32[]{:S(2)}, u32[]{:S(2)}) async-start(bf16[4,256,128]{2,1,0:T(8,128)(2,1)} %broadcast_select_fusion.1), calls=%async_computation.2 | async-start | bytes 524288 | tf_op jit(solution)/shard_map/all_to_all | solution.py:52
Sparse Core Ops, SparseCore 0:
  36.6 26.5 reduce-scatter.1
where the time goes:
time: 229 us; the launch traced here: 227 us
  waiting for transfers between devices  69.2 us (30%)
  local copies, waits for them, and re-layouts  43.5 us (19%)
  Pallas kernels  42 us (18%)
  other arithmetic  20.4 us (9%)
  blocking collectives  17.7 us (8%)
  between operations  13.5 us (6%)
  matrix products  10.6 us (5%)
  starting transfers between devices  9.72 us (4%)
    all_to_all x1, waiting for transfers between devices, body(): lax.all_to_all(outgoing, 'replica', split_axis=0, concat_axis=0, tiled=True)  59.8 us
    another operation x2, Pallas kernels  39.7 us
    psum x1, blocking collectives, body(): rank_total = lax.psum(partial_rank, 'tensor')  17.7 us
    unnamed x9, local copies, waits for them, and re-layouts  15.7 us
    gather x1, local copies, waits for them, and re-layouts, body(): pool_slot = jnp.take(adapter_slot_map, request_adapter)  12.6 us
    gather x1, local copies, waits for them, and re-layouts, body(): jnp.take(arrived.reshape(owners * capacity, quarter), sort_order, axis=0)  11.6 us
    all_to_all x1, waiting for transfers between devices, body(): lax.all_to_all(adapter_delta, 'replica', split_axis=0, concat_axis=0, til...  9.34 us
    all_to_all x1, starting transfers between devices, body(): lax.all_to_all(outgoing, 'replica', split_axis=0, concat_axis=0, tiled=True)  6.32 us
  transfers between devices with their start and end apart: 3, of which 2 were waited for; matrix products, arithmetic and copies ran while one was open for 23% of the time, Pallas kernels for 19%

commit v1 on v0

--- a/solution.py
+++ b/solution.py
@@ -1,12 +1,20 @@
+import functools
+
 import jax
 import jax.numpy as jnp
 from jax import lax
+from jax.experimental import pallas as pl
+from jax.experimental.pallas import tpu as pltpu
 from jax.sharding import PartitionSpec as P
 
 ADAPTER_SCALE = 0.5
-
-
-def body(tokens, value_weight, down_factor, up_factor, request_adapter, adapter_slot_map):
+MAX_OWNERS = 8
+VMEM_BYTES = 40 * 1024 * 1024
+NT = (((1,), (1,)), ((), ()))
+TN = (((0,), (0,)), ((), ()))
+
+
+def plain_body(tokens, value_weight, down_factor, up_factor, request_adapter, adapter_slot_map):
     row_count, quarter = tokens.shape
     owners = lax.axis_size("replica")
     local_adapters = down_factor.shape[0]
@@ -40,9 +48,7 @@
     partial_rank = lax.ragged_dot(
         rows_by_adapter, down_factor, group_row_count, preferred_element_type=jnp.float32
     )
-    rank_total = lax.psum(partial_rank, "tensor")
-    local_base_output = None
-    rank_projected = rank_total.astype(jnp.bfloat16)
+    rank_projected = lax.psum(partial_rank, "tensor").astype(jnp.bfloat16)
     sorted_delta = lax.ragged_dot(
         rank_projected, up_factor, group_row_count, preferred_element_type=jnp.float32
     ).astype(jnp.bfloat16)
@@ -58,6 +64,356 @@
     )
     local_base_output = lax.psum_scatter(partial_base, "tensor", scatter_dimension=1, tiled=True)
     return (local_base_output + ADAPTER_SCALE * adapter_delta_rows).astype(jnp.bfloat16)
+
+
+def iota(shape, dim):
+    return lax.broadcasted_iota(jnp.int32, shape, dim)
+
+
+def hot(mask):
+    return jnp.where(mask, 1.0, 0.0).astype(jnp.bfloat16)
+
+
+def lookup(request_ref, map_ref, owners, local_adapters):
+    rows, adapters = request_ref.shape[1], map_ref.shape[1]
+    slots = map_ref[...]
+    which = iota((16, adapters), 0)
+    owner = lax.div(slots, jnp.int32(local_adapters))
+    table = jnp.where(which == 8, slots, jnp.where(which == owner, 1, 0))
+    table = table.astype(jnp.float32).astype(jnp.bfloat16)
+    one_hot = hot(iota((adapters, rows), 0) == request_ref[...])
+    found = jnp.dot(table, one_hot, preferred_element_type=jnp.float32)
+    return found[8:9].astype(jnp.int32), found[0:8]
+
+
+def column_sums(table, counts):
+    wide = jnp.broadcast_to(counts, (counts.shape[0], 128)).astype(jnp.bfloat16)
+    return jnp.dot(table, wide, preferred_element_type=jnp.float32)[:, :1]
+
+
+def pack_kernel(
+    owners, local_adapters, me_ref, request_ref, map_ref, tokens_ref,
+    first_ref, over_ref, place_ref, branch_ref, packer_ref,
+):
+    rows = tokens_ref.shape[0]
+    capacity = 2 * rows // owners
+    half = capacity // 2
+    pool = map_ref.shape[1]
+
+    @pl.when(pl.program_id(0) == 0)
+    def _():
+        me = me_ref[0]
+        slots, marks = lookup(request_ref, map_ref, owners, local_adapters)
+        most = jnp.zeros((8, 1), jnp.float32)
+        slot = jnp.zeros((1, rows), jnp.int32)
+        for source in range(owners):
+            span = slice(source * rows, (source + 1) * rows)
+            most = jnp.maximum(most, jnp.sum(marks[:, span], axis=1, keepdims=True))
+            slot = jnp.where(me == source, slots[:, span], slot)
+        over = jnp.where(most > half, 1, 0)
+        branch = jnp.where(jnp.sum(over) <= 1, jnp.sum(over * iota((8, 1), 0)), owners)
+        branch_ref[0] = branch
+        mine = iota((pool, rows), 0) == slot
+        one_hot = hot(mine)
+        before = hot(iota((rows, rows), 0) < iota((rows, rows), 1))
+        ranks = jnp.dot(one_hot, before, preferred_element_type=jnp.float32)
+        counts = jnp.sum(jnp.where(mine, 1.0, 0.0), axis=1, keepdims=True)
+        row, column = iota((pool, pool), 0), iota((pool, pool), 1)
+        same = lax.div(row, jnp.int32(local_adapters)) == lax.div(column, jnp.int32(local_adapters))
+        ranks += column_sums(hot(same & (column < row)), counts)
+        rank = jnp.sum(jnp.where(mine, ranks, 0.0), axis=0, keepdims=True).astype(jnp.int32)
+        owner = lax.div(slot, jnp.int32(local_adapters))
+        place_ref[...] = jnp.broadcast_to(owner * capacity + rank, (8, rows))
+        first = jnp.where(rank < half, owner * half + rank, -1)
+        target = jnp.where(branch < owners, branch, me)
+        late = jnp.where((owner == target) & (rank >= half), rank - half, -1)
+        packer_ref[: owners * half, :] = hot(iota((owners * half, rows), 0) == first)
+        packer_ref[owners * half :, :] = hot(iota((half, rows), 0) == late)
+
+    packed = jnp.dot(packer_ref[...], tokens_ref[...], preferred_element_type=jnp.float32)
+    packed = packed.astype(jnp.bfloat16)
+    first_ref[...] = packed[: owners * half]
+    over_ref[...] = packed[owners * half :]
+
+
+def pack(me, requests, slot_map, tokens, owners, local_adapters):
+    rows, width = tokens.shape
+    half = rows // owners
+    pieces = 4
+    block = width // pieces
+    whole = lambda shape: pl.BlockSpec(shape, lambda i: (0, 0))
+    strip = lambda height: pl.BlockSpec((height, block), lambda i: (0, i))
+    return pl.pallas_call(
+        functools.partial(pack_kernel, owners, local_adapters),
+        grid=(pieces,),
+        in_specs=[
+            pl.BlockSpec(memory_space=pltpu.SMEM),
+            whole(requests.shape),
+            whole(slot_map.shape),
+            strip(rows),
+        ],
+        out_specs=[
+            strip(owners * half),
+            strip(half),
+            whole((8, rows)),
+            pl.BlockSpec(memory_space=pltpu.SMEM),
+        ],
+        out_shape=[
+            pltpu.HBM((owners * half, width), jnp.bfloat16),
+            pltpu.HBM((half, width), jnp.bfloat16),
+            jax.ShapeDtypeStruct((8, rows), jnp.int32),
+            jax.ShapeDtypeStruct((1,), jnp.int32),
+        ],
+        scratch_shapes=[pltpu.VMEM(((owners + 1) * half, rows), jnp.bfloat16)],
+        compiler_params=pltpu.CompilerParams(vmem_limit_bytes=VMEM_BYTES),
+        name="pack",
+    )(me, requests, slot_map, tokens)
+
+
+def plan_kernel(
+    owners, local_adapters, rows, me_ref, request_ref, map_ref, adapter_ref, bound_ref
+):
+    me = me_ref[0]
+    capacity = 2 * rows // owners
+    half = capacity // 2
+    slots, _ = lookup(request_ref, map_ref, owners, local_adapters)
+    row, column = iota((local_adapters, local_adapters), 0), iota((local_adapters, local_adapters), 1)
+    upto = hot(column <= row)
+    place = iota((local_adapters, capacity), 1)
+    for source in range(owners):
+        slot = slots[:, source * rows : (source + 1) * rows]
+        mine = iota((local_adapters, rows), 0) + me * local_adapters == slot
+        counts = jnp.sum(jnp.where(mine, 1.0, 0.0), axis=1, keepdims=True)
+        ends = column_sums(upto, counts).astype(jnp.int32)
+        passed = jnp.sum(jnp.where(ends <= place, 1, 0), axis=0, keepdims=True)
+        adapter = jnp.where(passed < local_adapters, passed, -1)
+        adapter = jnp.broadcast_to(adapter, (8, capacity))
+        adapter_ref[:, source * half : (source + 1) * half] = adapter[:, :half]
+        shift = lax.rem(me - source + owners, owners)
+        start = pl.multiple_of((owners + shift) * half, half)
+        adapter_ref[:, pl.ds(start, half)] = adapter[:, half:]
+    for part in range(2):
+        found = adapter_ref[:, part * owners * half : (part + 1) * owners * half]
+        bound_ref[2 * part] = jnp.min(jnp.where(found < 0, local_adapters, found))
+        bound_ref[2 * part + 1] = jnp.max(found)
+
+
+def plan(me, requests, slot_map, owners, local_adapters):
+    rows = requests.shape[1] // owners
+    vmem, smem = pl.BlockSpec(memory_space=pltpu.VMEM), pl.BlockSpec(memory_space=pltpu.SMEM)
+    return pl.pallas_call(
+        functools.partial(plan_kernel, owners, local_adapters, rows),
+        in_specs=[smem, vmem, vmem],
+        out_specs=[vmem, smem],
+        out_shape=[
+            jax.ShapeDtypeStruct((8, 2 * rows), jnp.int32),
+            jax.ShapeDtypeStruct((4,), jnp.int32),
+        ],
+        compiler_params=pltpu.CompilerParams(vmem_limit_bytes=VMEM_BYTES),
+        name="plan",
+    )(me, requests, slot_map)
+
+
+def down_kernel(part, rank, adapters, count, *refs):
+    bound_ref, adapter_ref, down_ref = refs[:3]
+    sent_refs = refs[3 : 3 + count]
+    total_ref, rows_ref, sems = refs[3 + count :]
+    step = pl.program_id(0)
+
+    @pl.when(step == 0)
+    def _():
+        size = sent_refs[0].shape[0]
+        copies = [
+            pltpu.make_async_copy(ref, rows_ref.at[k * size : (k + 1) * size], sems.at[k])
+            for k, ref in enumerate(sent_refs)
+        ]
+        for copy in copies:
+            copy.start()
+        total_ref[...] = jnp.zeros_like(total_ref)
+        for copy in copies:
+            copy.wait()
+
+    low = step * adapters
+
+    @pl.when((bound_ref[2 * part] < low + adapters) & (bound_ref[2 * part + 1] >= low))
+    def _():
+        products = lax.dot_general(
+            down_ref[...], rows_ref[...], NT, preferred_element_type=jnp.float32
+        )
+        total = total_ref[...]
+        for k in range(adapters):
+            chosen = adapter_ref[0:1, :] == low + k
+            total += jnp.where(chosen, products[k * rank : (k + 1) * rank], 0.0)
+        total_ref[...] = total
+
+
+def down(part, bounds, adapter_row, down_rows, sent, rank):
+    width = sent[0].shape[1]
+    slots = adapter_row.shape[1] // 2
+    adapters = 4
+    block = adapters * rank
+    return pl.pallas_call(
+        functools.partial(down_kernel, part, rank, adapters, len(sent)),
+        grid=(down_rows.shape[0] // block,),
+        in_specs=[
+            pl.BlockSpec(memory_space=pltpu.SMEM),
+            pl.BlockSpec((8, slots), lambda i: (0, part)),
+            pl.BlockSpec((block, width), lambda i: (i, 0)),
+        ]
+        + [pl.BlockSpec(memory_space=pl.ANY)] * len(sent),
+        out_specs=pl.BlockSpec((rank, slots), lambda i: (0, 0)),
+        out_shape=jax.ShapeDtypeStruct((rank, slots), jnp.float32),
+        scratch_shapes=[
+            pltpu.VMEM((slots, width), jnp.bfloat16),
+            pltpu.SemaphoreType.DMA((len(sent),)),
+        ],
+        compiler_params=pltpu.CompilerParams(vmem_limit_bytes=VMEM_BYTES),
+        cost_estimate=pl.CostEstimate(
+            flops=slots * width * down_rows.shape[0],
+            bytes_accessed=2 * width * (slots + down_rows.shape[0]),
+            transcendentals=0,
+        ),
+        name="down",
+    )(bounds, adapter_row, pltpu.with_memory_space_constraint(down_rows, pltpu.HBM), *sent)
+
+
+def up_kernel(owners, rank, adapters, me_ref, side_ref, adapter_ref, up_ref, mine_ref, other_ref, out_ref):
+    me, side = me_ref[0], side_ref[0]
+    mine, other = mine_ref[...].astype(jnp.float32), other_ref[...].astype(jnp.float32)
+    wide = mine.shape[1]
+    half = wide // owners
+    for part in range(2):
+        low_rank = jnp.where(side == part, mine, other)
+        chosen = adapter_ref[0:1, part * wide : (part + 1) * wide]
+        spread = jnp.concatenate(
+            [jnp.where(chosen == k, low_rank, 0.0).astype(jnp.bfloat16) for k in range(adapters)],
+            axis=0,
+        )
+        delta = lax.dot_general(up_ref[...], spread, TN, preferred_element_type=jnp.float32)
+        delta = delta.astype(jnp.bfloat16)
+        for k in range(owners):
+            source = k if part == 0 else lax.rem(me - k + owners, owners)
+            out_ref[source, :, part * half : (part + 1) * half] = delta[:, k * half : (k + 1) * half]
+
+
+def up(me, side, adapter_row, up_rows, mine, other, owners):
+    rank, wide = mine.shape
+    piece = up_rows.shape[1]
+    adapters = up_rows.shape[0] // rank
+    vmem, smem = pl.BlockSpec(memory_space=pltpu.VMEM), pl.BlockSpec(memory_space=pltpu.SMEM)
+    return pl.pallas_call(
+        functools.partial(up_kernel, owners, rank, adapters),
+        in_specs=[smem, smem, vmem, vmem, vmem, vmem],
+        out_shape=jax.ShapeDtypeStruct((owners, piece, 2 * wide // owners), jnp.bfloat16),
+        compiler_params=pltpu.CompilerParams(vmem_limit_bytes=VMEM_BYTES),
+        name="up",
+    )(me, side, adapter_row, up_rows, mine, other)
+
+
+def unpack_kernel(owners, place_ref, returned_ref, *refs):
+    base_refs, out_ref = refs[:-1], refs[-1]
+    rows, capacity = out_ref.shape[0], returned_ref.shape[2]
+    total = jnp.zeros((returned_ref.shape[1], rows), jnp.float32)
+    for owner in range(owners):
+        selector = hot(iota((capacity, rows), 0) == place_ref[0:1, :] - owner * capacity)
+        total += jnp.dot(returned_ref[owner], selector, preferred_element_type=jnp.float32)
+    base = base_refs[0][...]
+    for base_ref in base_refs[1:]:
+        base += base_ref[...]
+    out_ref[...] = (base + ADAPTER_SCALE * total.T).astype(jnp.bfloat16)
+
+
+def unpack(place, returned, base):
+    return pl.pallas_call(
+        functools.partial(unpack_kernel, returned.shape[0]),
+        out_shape=jax.ShapeDtypeStruct(base[0].shape, jnp.bfloat16),
+        compiler_params=pltpu.CompilerParams(vmem_limit_bytes=VMEM_BYTES),
+        name="unpack",
+    )(place, returned, *base)
+
+
+def exchange(array, axis, bit):
+    size = lax.axis_size(axis)
+    return lax.ppermute(array, axis, [(k, k ^ bit) for k in range(size)])
+
+
+def body(tokens, value_weight, down_factor, up_factor, request_adapter, adapter_slot_map):
+    row_count, quarter = tokens.shape
+    owners = lax.axis_size("replica")
+    tensor = lax.axis_size("tensor")
+    local_adapters, _, rank = down_factor.shape
+    half = row_count // owners
+    me = lax.axis_index("replica").astype(jnp.int32).reshape(1)
+    side = (lax.axis_index("tensor").astype(jnp.int32) % 2).reshape(1)
+    requests = request_adapter.reshape(1, -1)
+    slot_map = adapter_slot_map.reshape(1, -1)
+    down_rows = jnp.swapaxes(down_factor, 1, 2).reshape(local_adapters * rank, quarter)
+    up_rows = up_factor.reshape(local_adapters * rank, -1)
+
+    first, over, place, branch = pack(me, requests, slot_map, tokens, owners, local_adapters)
+    first = first.reshape(owners, half, quarter)
+    piece = value_weight.shape[1] // tensor
+
+    def work(late, first, over, tokens, value_weight, down_rows, requests, slot_map):
+        arrived = lax.all_to_all(first, "replica", split_axis=0, concat_axis=0, tiled=True)
+        base = []
+        for bit in range(tensor):
+            column = (lax.axis_index("tensor") ^ bit) * piece
+            part = jnp.dot(
+                tokens,
+                lax.dynamic_slice_in_dim(value_weight, column, piece, 1),
+                preferred_element_type=jnp.float32,
+            )
+            base.append(part if bit == 0 else exchange(part, "tensor", bit))
+        adapter_row, bounds = plan(me, requests, slot_map, owners, local_adapters)
+        one = down(
+            0, bounds, adapter_row, down_rows, (arrived.reshape(owners * half, quarter),), rank
+        )
+        two = down(1, bounds, adapter_row, down_rows, (over, *late), rank)
+        return one, two, adapter_row, *base
+
+    def to_one(owner):
+        def send(place, first, over, tokens, *rest):
+            late = tuple(
+                lax.ppermute(over, "replica", [((owner - shift) % owners, owner)])
+                for shift in range(1, owners)
+            )
+            return work(late, first, over, tokens, *rest)
+
+        return send
+
+    def to_all(place, first, over, tokens, *rest):
+        spot = place[0]
+        owner, late = spot // (2 * half), spot % (2 * half) - half
+        index = jnp.where(late >= 0, owner * half + late, -1)
+        packer = (jnp.arange(owners * half)[:, None] == index[None, :]).astype(jnp.bfloat16)
+        outgoing = jnp.dot(packer, tokens, preferred_element_type=jnp.float32)
+        outgoing = outgoing.astype(jnp.bfloat16).reshape(owners, half, quarter)
+        came = lax.all_to_all(outgoing, "replica", split_axis=0, concat_axis=0, tiled=True)
+        here = lax.axis_index("replica")
+        late = tuple(
+            lax.dynamic_index_in_dim(came, (here - shift) % owners, 0, keepdims=False)
+            for shift in range(1, owners)
+        )
+        return work(late, first, over, tokens, *rest)
+
+    one, two, adapter_row, *base = lax.switch(
+        branch[0],
+        [to_one(owner) for owner in range(owners)] + [to_all],
+        place, first, over, tokens, value_weight, down_rows, requests, slot_map,
+    )
+    keep = jnp.where(side[0] == 0, one, two)
+    give = jnp.where(side[0] == 0, two, one)
+    keep = keep + exchange(give, "tensor", 1)
+    bit = 2
+    while bit < tensor:
+        keep = keep + exchange(keep, "tensor", bit)
+        bit *= 2
+    mine = keep.astype(jnp.bfloat16)
+    other = exchange(mine, "tensor", 1)
+    delta = up(me, side, adapter_row, up_rows, mine, other, owners)
+    returned = lax.all_to_all(delta, "replica", split_axis=0, concat_axis=0, tiled=True)
+    return unpack(place, returned, base)
 
 
 def solution(mesh):
@@ -70,4 +426,5 @@
         P("parts"),
     )
     out_specs = P(("parts", "replica"), "tensor")
-    return jax.shard_map(body, mesh=mesh, in_specs=in_specs, out_specs=out_specs, check_vma=False)
+    chosen = body if mesh.shape["replica"] <= MAX_OWNERS else plain_body
+    return jax.shard_map(chosen, mesh=mesh, in_specs=in_specs, out_specs=out_specs, check_vma=False)

time: 229 us -> 125 us (0.55)
  waiting for transfers between devices: 69.2 us -> 22 us
  local copies, waits for them, and re-layouts: 43.5 us -> 6.26 us
  other arithmetic: 20.4 us -> 0.07 us
  blocking collectives: 17.7 us -> 37.9 us
  Pallas kernels: 42 us -> 26.7 us
  between operations: 13.5 us -> 0.73 us
  starting transfers between devices: 9.72 us -> 19.1 us
    all_to_all x2 -> x1, waiting for transfers between devices: 69.1 us -> 0.01 us  [work(): lax.all_to_all(first, 'replica', split_axis=0, concat_axis=0, tiled=True)]
    another operation x2 -> x0, Pallas kernels: 39.7 us -> none
    all_to_all x0 -> x1, blocking collectives: none -> 37.9 us  [body(): lax.all_to_all(delta, 'replica', split_axis=0, concat_axis=0, tiled=True)]
    gather x3 -> x0, local copies, waits for them, and re-layouts: 27.4 us -> none  [the longest x1 12.6 us: body(): pool_slot = jnp.take(adapter_slot_map, request_adapter)]
    pallas_call x0 -> x6, Pallas kernels: none -> 26.7 us  [the longest x2 16.1 us: down(): pl.pallas_call(functools.partial(down_kernel, part, rank, adapters, len(s...]
    ppermute x0 -> x9, waiting for transfers between devices: none -> 22 us  [the longest x3 14.1 us: send(): lax.ppermute(over, 'replica', [((owner - shift) % owners, owner)])]
    psum x1 -> x0, blocking collectives: 17.7 us -> none  [body(): rank_total = lax.psum(partial_rank, 'tensor')]
    unnamed x9 -> x6, local copies, waits for them, and re-layouts: 15.7 us -> 0.01 us
  transfers between devices with their start and end apart: 3 -> 10, of which waited for: 2 -> 5; matrix products, arithmetic and copies ran while one was open for 23% -> 14% of each run, Pallas kernels for 19% -> 7%
where the time goes in v1:
time: 125 us
  blocking collectives  37.9 us (30%)
  Pallas kernels  26.7 us (21%)
  waiting for transfers between devices  22 us (18%)
  starting transfers between devices  19.1 us (15%)
  matrix products  11.3 us (9%)
  local copies, waits for them, and re-layouts  6.26 us (5%)
    all_to_all x1, blocking collectives, body(): lax.all_to_all(delta, 'replica', split_axis=0, concat_axis=0, tiled=True)  37.9 us
    pallas_call x2, Pallas kernels, down(): pl.pallas_call(functools.partial(down_kernel, part, rank, adapters, len(s...  16.1 us
    ppermute x3, waiting for transfers between devices, send(): lax.ppermute(over, 'replica', [((owner - shift) % owners, owner)])  14.1 us
    dot_general x4, matrix products, work(): jnp.dot(tokens, lax.dynamic_slice_in_dim(value_weight, column, piece, 1),...  11.3 us
    ppermute x3, starting transfers between devices, send(): lax.ppermute(over, 'replica', [((owner - shift) % owners, owner)])  9.13 us
    ppermute x6, waiting for transfers between devices, exchange(): return lax.ppermute(array, axis, [(k, k ^ bit) for k in range(size)])  7.93 us
    all_to_all x1, starting transfers between devices, work(): lax.all_to_all(first, 'replica', split_axis=0, concat_axis=0, tiled=True)  6.33 us
    cond x4, local copies, waits for them, and re-layouts, body(): lax.switch(branch[0], [to_one(owner) for owner in range(owners)] + [to_al...  6.24 us
  transfers between devices with their start and end apart: 10, of which 5 were waited for; matrix products, arithmetic and copies ran while one was open for 14% of the time, Pallas kernels for 7%

profile of v1, /device:TPU:0, one launch (start us, length us, event | category | flops | bytes accessed | tf_op | source)
XLA Modules:
  0.0 124.7 jit_solution(18442067538939112912)
XLA Ops:
  0.0 0.0 copy-start.6
  0.0 0.0 copy-start.7
  0.0 5.6 %pack.1 = (bf16[512,2048]{1,0:T(8,128)(2,1)}, bf16[128,2048]{1,0:T(8,128)(2,1)}, s32[8,512]{1,0:T(8,128)S(1)}, s32[1]{0:T(128)}) custom-call(s32[1]{0:T(128)} %bitcast.30.me_ref, s32[1,2048]{1,0:T(1,128)} %bitcast.101, s32[1,128]{1,0:T(1,128)} %bitcast.107, bf16[512,2048]{1,0:T(8,128)(2,1)} %tokens_ref.1), custom_call_target="tpu_custom_call" | custom-call | tf_op jit(solution)/shard_map/pack/pallas_call | solution.py:146
  6.3 0.0 copy-done.6
  6.3 0.0 copy-done.7
  6.3 0.0 copy-start
  6.3 68.2 %conditional.1 = (f32[64,512]{1,0:T(8,128)S(1)}, f32[64,512]{1,0:T(8,128)S(1)}, s32[8,1024]{1,0:T(8,128)}, f32[512,128]{1,0:T(8,128)}, f32[512,128]{1,0:T(8,128)...) conditional(s32[]{:T(128)} %bitcast.34, (s32[1]{0:T(128)}, s32[1,2048]{1,0:T(1,128)S(1)}, ...), branch_computations={%region_0.1_spmd, %region_1.2_spmd, %region_2.3_spmd, %region_3.4_... | conditional | flops 6443773952 | bytes 59775980 | solution.py:400
  6.6 6.3 %all-to-all-start.3 = ((bf16[4,128,2048]{2,1,0:T(8,128)(2,1)}), bf16[4,128,2048]{2,1,0:T(8,128)(2,1)S(1)}, u32[]{:S(2)}, u32[]{:S(2)}) async-start(bf16[4,128,2048]{2,1,0:T(8,128)(2,1)} %get-tuple-element.123), calls=%async_computation.3 | async-start | bytes 4194304 | tf_op jit(solution)/shard_map/cond/branch_3_fun/all_to_all | solution.py:358
  12.9 0.7 collective-permute-start.18
  13.6 1.5 %collective-permute-start.19 = (bf16[128,2048]{1,0:T(8,128)(2,1)}, bf16[128,2048]{1,0:T(8,128)(2,1)}, u32[]{:S(2)}, u32[]{:S(2)}) collective-permute-start(bf16[128,2048]{1,0:T(8,128)(2,1)} %get-tuple-element.124.refs_3_), channel_id=1, source_target_pairs={{4,12},{5,13},{6,14},{7,15},{20,28},{21,29},{22,30},{23,31}} | collective-permute-start | bytes 1572872 | tf_op jit(solution)/shard_map/cond/branch_3_fun/ppermute | solution.py:378
  15.1 7.0 %collective-permute-start.20 = (bf16[128,2048]{1,0:T(8,128)(2,1)}, bf16[128,2048]{1,0:T(8,128)(2,1)}, u32[]{:S(2)}, u32[]{:S(2)}) collective-permute-start(bf16[128,2048]{1,0:T(8,128)(2,1)} %get-tuple-element.124.refs_3_), channel_id=1, source_target_pairs={{0,12},{1,13},{2,14},{3,15},{16,28},{17,29},{18,30},{19,31}} | collective-permute-start | bytes 1572872 | tf_op jit(solution)/shard_map/cond/branch_3_fun/ppermute | solution.py:378
  22.1 2.6 %convolution_bitcast_fusion.14 = f32[512,128]{0,1:T(8,128)S(1)} fusion(bf16[512,2048]{1,0:T(8,128)(2,1)} %get-tuple-element.126, bf16[2048,512]{1,0:T(8,128)(2,1)} %get-tuple-element.125, s32[]{:T(128)S(6)} %select_n.99), kind=kOutput, calls=%fused_computation.38 | convolution fusion | flops 268435456 | bytes 2883588 | tf_op jit(solution)/shard_map/cond/branch_3_fun/dot_general | solution.py:362
  24.7 0.1 collective-permute-start.21
  24.8 3.3 %convolution_bitcast_fusion.13 = f32[512,128]{0,1:T(8,128)} fusion(bf16[512,2048]{1,0:T(8,128)(2,1)} %get-tuple-element.126, bf16[2048,512]{1,0:T(8,128)(2,1)} %get-tuple-element.125, s32[]{:T(128)S(6)} %select_n.100), kind=kOutput, calls=%fused_computation.37 | convolution fusion | flops 268435456 | bytes 2883588 | tf_op jit(solution)/shard_map/cond/branch_3_fun/dot_general | solution.py:362
  28.1 1.5 %collective-permute-start.22 = (f32[512,128]{0,1:T(8,128)}, f32[512,128]{0,1:T(8,128)}, u32[]{:S(2)}, u32[]{:S(2)}) collective-permute-start(f32[512,128]{0,1:T(8,128)} %convolution_bitcast_fusion.13), channel_id=1, source_target_pairs={{0,2},{1,3},{2,0},{3,1},{4,6},{5,7},{6,4},{7,5},{8,10},{9,11},{10,... | collective-permute-start | bytes 786440 | tf_op jit(solution)/shard_map/cond/branch_3_fun/ppermute | solution.py:337
  29.6 0.0 copy-start.4
  29.6 3.5 %convolution_bitcast_fusion.12 = f32[512,128]{0,1:T(8,128)} fusion(bf16[512,2048]{1,0:T(8,128)(2,1)} %get-tuple-element.126, bf16[2048,512]{1,0:T(8,128)(2,1)} %get-tuple-element.125, s32[]{:T(128)S(6)} %select_n.101), kind=kOutput, calls=%fused_computation.36 | convolution fusion | flops 268435456 | bytes 2883588 | tf_op jit(solution)/shard_map/cond/branch_3_fun/dot_general | solution.py:362
  33.1 0.0 collective-permute-done.21
  33.1 0.3 collective-permute-start.23
  33.4 0.0 copy-done.4
  33.4 1.9 %convolution_bitcast_fusion.15 = f32[512,128]{0,1:T(8,128)S(1)} fusion(bf16[512,2048]{1,0:T(8,128)(2,1)S(1)} %copy-done.4, bf16[2048,512]{1,0:T(8,128)(2,1)} %get-tuple-element.125, s32[]{:T(128)S(6)} %select_n.98), kind=kOutput, calls=%fused_computation.39 | convolution fusion | flops 268435456 | bytes 2883588 | tf_op jit(solution)/shard_map/cond/branch_3_fun/dot_general | solution.py:362
  35.3 0.8 copy.14
  36.1 1.3 %plan.8 = (s32[8,1024]{1,0:T(8,128)}, s32[4]{0:T(128)S(1)}) custom-call(s32[1]{0:T(128)} %get-tuple-element.117.me_ref, s32[1,2048]{1,0:T(1,128)S(1)} %get-tuple-element.118.request_ref, s32[1,128]{1,0:T(1,128)S(1)} %get-tuple-element.119.map_ref), custom_call_target="tpu_custom_call" | custom-call | tf_op jit(solution)/shard_map/cond/branch_3_fun/plan/pallas_call | solution.py:204
  37.4 1.8 %copy.19 = f32[512,128]{1,0:T(8,128)} copy(f32[512,128]{0,1:T(8,128)} %collective-permute-done.21) | data formatting | bytes 524288 | tf_op jit(solution)/shard_map/cond | solution.py:400
  39.2 0.0 collective-permute-done.22
  39.2 1.8 %copy.24 = f32[512,128]{1,0:T(8,128)} copy(f32[512,128]{0,1:T(8,128)} %collective-permute-done.22) | data formatting | bytes 524288 | tf_op jit(solution)/shard_map/cond | solution.py:400
  41.0 1.3 %collective-permute-done.23 = f32[512,128]{0,1:T(8,128)} collective-permute-done((f32[512,128]{0,1:T(8,128)}, f32[512,128]{0,1:T(8,128)}, u32[]{:S(2)}, u32[]{:S(2)}) %collective-permute-start.23) | collective-permute-done | bytes 262176 | tf_op jit(solution)/shard_map/cond/branch_3_fun/ppermute | solution.py:337
  42.3 1.8 %copy.29 = f32[512,128]{1,0:T(8,128)} copy(f32[512,128]{0,1:T(8,128)} %collective-permute-done.23) | data formatting | bytes 524288 | tf_op jit(solution)/shard_map/cond | solution.py:400
  44.1 0.0 collective-permute-done.18.refs_4_
  44.1 0.0 collective-permute-done.19.refs_5_
  44.1 14.1 %collective-permute-done.20.refs_6_ = bf16[128,2048]{1,0:T(8,128)(2,1)} collective-permute-done((bf16[128,2048]{1,0:T(8,128)(2,1)}, bf16[128,2048]{1,0:T(8,128)(2,1)}, u32[]{:S(2)}, u32[]{:S(2)}) %collective-permute-start.20) | collective-permute-done | bytes 524320 | tf_op jit(solution)/shard_map/cond/branch_3_fun/ppermute | solution.py:378
  58.2 6.9 %down.17 = f32[64,512]{1,0:T(8,128)S(1)} custom-call(s32[4]{0:T(128)S(1)} %get-tuple-element.120.refs_0_, s32[8,1024]{1,0:T(8,128)} %get-tuple-element.190.refs_1_, bf16[2048,2048]{1,0:T(8,128)(2,1)} %get-tuple-element.122.refs_2_, bf16[128,2048]{1,0:T(8,128)(2,1)} %get-tuple-element.124.refs_3_, bf16[128,2048]{1,0:T(8,128)(2,1)S(1)} %collective-permute-done.18.refs_4_, ...), custom_call_target="tpu_custom_call" | custom-call | flops 2147483648 | bytes 10485760 | tf_op jit(solution)/shard_map/cond/branch_3_fun/down/pallas_call | solution.py:255
  65.2 0.0 all-to-all-done.3
  65.2 9.2 %down.16 = f32[64,512]{1,0:T(8,128)S(1)} custom-call(s32[4]{0:T(128)S(1)} %get-tuple-element.120.refs_0_, s32[8,1024]{1,0:T(8,128)} %get-tuple-element.190.refs_1_, bf16[2048,2048]{1,0:T(8,128)(2,1)} %get-tuple-element.122.refs_2_, bf16[512,2048]{1,0:T(8,128)(2,1)S(1)} %bitcast.88), custom_call_target="tpu_custom_call" | custom-call | flops 2147483648 | bytes 10485760 | tf_op jit(solution)/shard_map/cond/branch_3_fun/down/pallas_call | solution.py:255
  74.6 0.1 collective-permute-start.27
  74.7 1.3 %collective-permute-done.27 = f32[64,512]{1,0:T(8,128)S(1)} collective-permute-done((f32[64,512]{1,0:T(8,128)S(1)}, f32[64,512]{1,0:T(8,128)S(1)}, u32[]{:S(2)}, u32[]{:S(2)}) %collective-permute-start.27) | collective-permute-done | bytes 131104 | tf_op jit(solution)/shard_map/ppermute | solution.py:337
  76.0 1.6 %collective-permute-start.28 = (f32[64,512]{1,0:T(8,128)S(1)}, f32[64,512]{1,0:T(8,128)S(1)}, u32[]{:S(2)}, u32[]{:S(2)}) collective-permute-start(f32[64,512]{1,0:T(8,128)S(1)} %select_add_fusion), channel_id=1, source_target_pairs={{0,2},{1,3},{2,0},{3,1},{4,6},{5,7},{6,4},{7,5},{8,10},{9,11},{10,... | collective-permute-start | bytes 393224 | tf_op jit(solution)/shard_map/ppermute | solution.py:337
  77.6 4.1 %collective-permute-done.28 = f32[64,512]{1,0:T(8,128)S(1)} collective-permute-done((f32[64,512]{1,0:T(8,128)S(1)}, f32[64,512]{1,0:T(8,128)S(1)}, u32[]{:S(2)}, u32[]{:S(2)}) %collective-permute-start.28) | collective-permute-done | bytes 131104 | tf_op jit(solution)/shard_map/ppermute | solution.py:337
  81.7 0.1 collective-permute-start.29
  81.8 1.2 collective-permute-done.29.other_ref
  83.0 0.0 copy-done
  83.0 1.5 %up.1 = bf16[4,128,256]{2,1,0:T(8,128)(2,1)S(1)} custom-call(s32[1]{0:T(128)} %bitcast.30.me_ref, s32[1]{0:T(128)} %bitcast.33.side_ref, s32[8,1024]{1,0:T(8,128)} %get-tuple-element.153.adapter_ref, bf16[2048,128]{1,0:T(8,128)(2,1)S(1)} %bitcast.89, bf16[64,512]{1,0:T(8,128)(2,1)S(1)} %add_convert_fusion.mine_ref, ...), custom_call_target="tpu_custom_call" | custom-call | tf_op jit(solution)/shard_map/up/pallas_call | solution.py:304
  84.5 37.9 %all_to_all.29.returned_ref = bf16[4,128,256]{2,1,0:T(8,128)(2,1)S(1)} all-to-all(bf16[4,128,256]{2,1,0:T(8,128)(2,1)S(1)} %up.1), channel_id=1, replica_groups=mesh['parts'=2,'replica'=4,'tensor'=4] {'replica'}, dimensions={0} | all-to-all | bytes 524288 | tf_op jit(solution)/shard_map/all_to_all | solution.py:415
  122.4 2.3 %unpack.1 = bf16[512,128]{1,0:T(8,128)(2,1)} custom-call(s32[8,512]{1,0:T(8,128)S(1)} %get-tuple-element.149.place_ref, bf16[4,128,256]{2,1,0:T(8,128)(2,1)S(1)} %all_to_all.29.returned_ref, f32[512,128]{1,0:T(8,128)} %get-tuple-element.160.refs_0_, f32[512,128]{1,0:T(8,128)} %get-tuple-element.161.refs_1_, f32[512,128]{1,0:T(8,128)} %get-tuple-element.162.refs_2_, ...), custom_call_target="tpu_custom_call" | custom-call | tf_op jit(solution)/shard_map/unpack/pallas_call | solution.py:327
  (3 shorter events, 0.1 us)
Async XLA Ops:
  0.0 6.3 %copy-start.6 = (s32[2048]{0:T(1024)S(1)}, s32[2048]{0:T(1024)}, u32[]{:S(2)}) copy-start(s32[2048]{0:T(1024)} %param.15) | copy-start | bytes 24580
  0.0 6.3 %copy-start.7 = (s32[128]{0:T(128)S(1)}, s32[128]{0:T(128)}, u32[]{:S(2)}) copy-start(s32[128]{0:T(128)} %param.16) | copy-start | bytes 1540
  6.3 76.7 %copy-start = (bf16[32,64,128]{2,1,0:T(8,128)(2,1)S(1)}, bf16[32,64,128]{2,1,0:T(8,128)(2,1)}, u32[]{:S(2)}) copy-start(bf16[32,64,128]{2,1,0:T(8,128)(2,1)} %param.14) | copy-start | bytes 1572868
  6.6 58.6 %all-to-all-start.3 = ((bf16[4,128,2048]{2,1,0:T(8,128)(2,1)}), bf16[4,128,2048]{2,1,0:T(8,128)(2,1)S(1)}, u32[]{:S(2)}, u32[]{:S(2)}) async-start(bf16[4,128,2048]{2,1,0:T(8,128)(2,1)} %get-tuple-element.123), calls=%async_computation.3 | async-start | bytes 4194304 | tf_op jit(solution)/shard_map/cond/branch_3_fun/all_to_all | solution.py:358
  12.9 31.2 %collective-permute-start.18 = (bf16[128,2048]{1,0:T(8,128)(2,1)}, bf16[128,2048]{1,0:T(8,128)(2,1)S(1)}, u32[]{:S(2)}, u32[]{:S(2)}) collective-permute-start(bf16[128,2048]{1,0:T(8,128)(2,1)} %get-tuple-element.124.refs_3_), channel_id=1, source_target_pairs={{8,12},{9,13},{10,14},{11,15},{24,28},{25,29},{26,30},{27,31}} | collective-permute-start | bytes 1572872 | tf_op jit(solution)/shard_map/cond/branch_3_fun/ppermute | solution.py:378
  13.6 30.5 %collective-permute-start.19 = (bf16[128,2048]{1,0:T(8,128)(2,1)}, bf16[128,2048]{1,0:T(8,128)(2,1)}, u32[]{:S(2)}, u32[]{:S(2)}) collective-permute-start(bf16[128,2048]{1,0:T(8,128)(2,1)} %get-tuple-element.124.refs_3_), channel_id=1, source_target_pairs={{4,12},{5,13},{6,14},{7,15},{20,28},{21,29},{22,30},{23,31}} | collective-permute-start | bytes 1572872 | tf_op jit(solution)/shard_map/cond/branch_3_fun/ppermute | solution.py:378
  15.1 43.1 %collective-permute-start.20 = (bf16[128,2048]{1,0:T(8,128)(2,1)}, bf16[128,2048]{1,0:T(8,128)(2,1)}, u32[]{:S(2)}, u32[]{:S(2)}) collective-permute-start(bf16[128,2048]{1,0:T(8,128)(2,1)} %get-tuple-element.124.refs_3_), channel_id=1, source_target_pairs={{0,12},{1,13},{2,14},{3,15},{16,28},{17,29},{18,30},{19,31}} | collective-permute-start | bytes 1572872 | tf_op jit(solution)/shard_map/cond/branch_3_fun/ppermute | solution.py:378
  24.7 8.4 %collective-permute-start.21 = (f32[512,128]{0,1:T(8,128)S(1)}, f32[512,128]{0,1:T(8,128)}, u32[]{:S(2)}, u32[]{:S(2)}) collective-permute-start(f32[512,128]{0,1:T(8,128)S(1)} %convolution_bitcast_fusion.14), channel_id=1, source_target_pairs={{0,1},{1,0},{2,3},{3,2},{4,5},{5,4},{6,7},{7,6},{8,9},{9,8},{10,11... | collective-permute-start | bytes 786440 | tf_op jit(solution)/shard_map/cond/branch_3_fun/ppermute | solution.py:337
  28.1 11.1 %collective-permute-start.22 = (f32[512,128]{0,1:T(8,128)}, f32[512,128]{0,1:T(8,128)}, u32[]{:S(2)}, u32[]{:S(2)}) collective-permute-start(f32[512,128]{0,1:T(8,128)} %convolution_bitcast_fusion.13), channel_id=1, source_target_pairs={{0,2},{1,3},{2,0},{3,1},{4,6},{5,7},{6,4},{7,5},{8,10},{9,11},{10,... | collective-permute-start | bytes 786440 | tf_op jit(solution)/shard_map/cond/branch_3_fun/ppermute | solution.py:337
  29.6 3.8 %copy-start.4 = (bf16[512,2048]{1,0:T(8,128)(2,1)S(1)}, bf16[512,2048]{1,0:T(8,128)(2,1)}, u32[]{:S(2)}) copy-start(bf16[512,2048]{1,0:T(8,128)(2,1)} %get-tuple-element.126) | copy-start | bytes 6291460 | tf_op jit(solution)/shard_map/cond
  33.1 9.2 %collective-permute-start.23 = (f32[512,128]{0,1:T(8,128)}, f32[512,128]{0,1:T(8,128)}, u32[]{:S(2)}, u32[]{:S(2)}) collective-permute-start(f32[512,128]{0,1:T(8,128)} %convolution_bitcast_fusion.12), channel_id=1, source_target_pairs={{0,3},{1,2},{2,1},{3,0},{4,7},{5,6},{6,5},{7,4},{8,11},{9,10},{10,... | collective-permute-start | bytes 786440 | tf_op jit(solution)/shard_map/cond/branch_3_fun/ppermute | solution.py:337
  74.6 1.4 %collective-permute-start.27 = (f32[64,512]{1,0:T(8,128)S(1)}, f32[64,512]{1,0:T(8,128)S(1)}, u32[]{:S(2)}, u32[]{:S(2)}) collective-permute-start(f32[64,512]{1,0:T(8,128)S(1)} %broadcast_select_fusion), channel_id=1, source_target_pairs={{0,1},{1,0},{2,3},{3,2},{4,5},{5,4},{6,7},{7,6},{8,9},{9,8},{10,11... | collective-permute-start | bytes 393224 | tf_op jit(solution)/shard_map/ppermute | solution.py:337
  76.0 5.6 %collective-permute-start.28 = (f32[64,512]{1,0:T(8,128)S(1)}, f32[64,512]{1,0:T(8,128)S(1)}, u32[]{:S(2)}, u32[]{:S(2)}) collective-permute-start(f32[64,512]{1,0:T(8,128)S(1)} %select_add_fusion), channel_id=1, source_target_pairs={{0,2},{1,3},{2,0},{3,1},{4,6},{5,7},{6,4},{7,5},{8,10},{9,11},{10,... | collective-permute-start | bytes 393224 | tf_op jit(solution)/shard_map/ppermute | solution.py:337
  81.7 1.3 %collective-permute-start.29 = (bf16[64,512]{1,0:T(8,128)(2,1)S(1)}, bf16[64,512]{1,0:T(8,128)(2,1)S(1)}, u32[]{:S(2)}, u32[]{:S(2)}) collective-permute-start(bf16[64,512]{1,0:T(8,128)(2,1)S(1)} %add_convert_fusion.mine_ref), channel_id=1, source_target_pairs={{0,1},{1,0},{2,3},{3,2},{4,5},{5,4},{6,7},{7,6},{8,9},{9,8},{10,11... | collective-permute-start | bytes 196616 | tf_op jit(solution)/shard_map/ppermute | solution.py:337
